TPU v7x, 128 devices: a whole 4x4x4 slice. The times are simulated.
128 devices in a mesh: blk: 16 (over x, z_lo, core), uly: 8 (over z_hi, y).
Axes of the slice: x: 4, y: 4, z: 4 (z_hi: 2, z_lo: 2; z = z_hi * 2 + z_lo), core: 2. Of those that a mesh axis runs over, the one named last changes fastest.
Arguments:
- activations: bfloat16 [12288, 4096], P(('blk', 'uly')), may hold values from -64 to 64
- input_norm_gain: float32 [4096], replicated, may hold values from 0.5 to 2
- query_weight: bfloat16 [4096, 4096], P(None, 'uly'), may hold values from -3 to 3
- key_weight: bfloat16 [4096, 1024], P(None, 'uly'), may hold values from -3 to 3
- value_weight: bfloat16 [4096, 1024], P(None, 'uly'), may hold values from -0.09375 to 0.09375
- output_weight: bfloat16 [4096, 4096], P('uly'), may hold values from -1 to 1
- adapter_down_maps: bfloat16 [4096, 384], replicated, may hold values from -0.09375 to 0.09375
- query_up_maps: bfloat16 [128, 4096], P(None, 'uly'), may hold values from -0.375 to 0.375
- key_up_maps: bfloat16 [128, 1024], P(None, 'uly'), may hold values from -0.375 to 0.375
- value_up_maps: bfloat16 [128, 1024], P(None, 'uly'), may hold values from -0.375 to 0.375
- output_down_maps: bfloat16 [4096, 128], P('uly'), may hold values from -0.5 to 0.5
- output_up_maps: bfloat16 [128, 4096], replicated, may hold values from -1.5 to 1.5
- segment_index: int32 [12288], replicated, may hold values from 0 to 3, never falling along the last dimension, each value on 1 to 9216 neighbouring positions
- segment_adapter: int32 [4], replicated, may hold values from 0 to 7
Outputs:
- attn_out: bfloat16 [12288, 4096], P(('blk', 'uly'))
Inputs may be any that keep to these rules, and one draw needn't show every extreme that they name: `segment_index`: never falling along the sequence; each of the 4 segments covers 1 to 9216 tokens, and one covers exactly that many. `segment_adapter`: one adapter per segment; segments may share one.
All inputs are finite; a program needn't handle non-finite values.
Results may differ from a plain program's by a relative error of at most 0.019.
The roundings to bfloat16 on the way count: a program that leaves them out, or rounds other values in their place, can miss the bound.
Values may be sent and summed in bfloat16 or wider, within the bound.
No kernel may reach another device: no remote copies, remote signals or barrier semaphores. Data moves between devices by JAX's collectives and lax.ppermute only.
A program may use at most 192 MiB of HBM per device.

v0:
```python
import math

import jax
import jax.numpy as jnp
from jax import lax
from jax.sharding import PartitionSpec as P

QUERY_HEADS = 32
KEY_VALUE_HEADS = 8
HEAD_SIZE = 128
ADAPTER_RANK = 16
ADAPTER_COUNT = 8


eps_norm = 1e-05
adapter_scale = 2.0


def tenant_rows(seg_rows, segment_adapter):
    match = seg_rows[:, None] == jnp.arange(segment_adapter.shape[0], dtype=jnp.int32)[None, :]
    return jnp.sum(jnp.where(match, segment_adapter[None, :], 0), axis=1)


def normalize(activations, input_norm_gain):
    values = activations.astype(jnp.float32)
    power = jnp.mean(values * values, axis=1, keepdims=True)
    return (values * lax.rsqrt(power + eps_norm) * input_norm_gain[None, :]).astype(jnp.bfloat16)


def tenant_adapter_mask(tenant_index, hidden_width):
    columns = jnp.arange(hidden_width, dtype=jnp.int32) // ADAPTER_RANK % ADAPTER_COUNT
    return columns[None, :] == tenant_index[:, None]


def attend_local(query_rows, key_matrix_rows, value_matrix_rows, query_pos, segment_index):
    total_rows = query_rows.shape[0]
    kv_heads = key_matrix_rows.shape[1] // HEAD_SIZE
    query_group = QUERY_HEADS // KEY_VALUE_HEADS
    score_scale = 1.0 / math.sqrt(HEAD_SIZE)
    query_matrix = query_rows.reshape(total_rows, kv_heads, query_group, HEAD_SIZE)
    query_seg = jnp.take(segment_index, query_pos)
    last_query = jnp.max(query_pos)
    init = (
        jnp.full((total_rows, kv_heads, query_group), -1e30, jnp.float32),
        jnp.zeros((total_rows, kv_heads, query_group), jnp.float32),
        jnp.zeros((total_rows, kv_heads, query_group, HEAD_SIZE), jnp.float32),
    )
    key_piece = lax.all_gather(key_matrix_rows, "blk", axis=0, tiled=True)
    value_piece = lax.all_gather(value_matrix_rows, "blk", axis=0, tiled=True)
    count = key_piece.shape[0]
    step = math.gcd(count, 512)

    def visit(index, state):
        offset = index * step

        def compute(inner):
            peak, total, summed = inner
            key_block = lax.dynamic_slice_in_dim(key_piece, offset, step).reshape(
                step, kv_heads, HEAD_SIZE
            )
            value_block = lax.dynamic_slice_in_dim(value_piece, offset, step).reshape(
                step, kv_heads, HEAD_SIZE
            )
            key_pos = offset + jnp.arange(step, dtype=jnp.int32)
            key_seg = lax.dynamic_slice_in_dim(segment_index, offset, step)
            allowed = (key_pos[None, :] <= query_pos[:, None]) & (
                key_seg[None, :] == query_seg[:, None]
            )
            allowed = allowed[:, None, None, :]
            scores = (
                jnp.einsum(
                    "rkgd,nkd->rkgn", query_matrix, key_block, preferred_element_type=jnp.float32
                )
                * score_scale
            )
            fresh = jnp.maximum(peak, jnp.max(jnp.where(allowed, scores, -1e30), axis=3))
            weights = jnp.where(allowed, jnp.exp(scores - fresh[..., None]), 0.0)
            decay = jnp.exp(peak - fresh)
            total = total * decay + jnp.sum(weights, axis=3)
            summed = summed * decay[..., None] + jnp.einsum(
                "rkgn,nkd->rkgd",
                weights.astype(jnp.bfloat16),
                value_block,
                preferred_element_type=jnp.float32,
            )
            return (fresh, total, summed)

        return lax.cond(offset <= last_query, compute, lambda inner: inner, state)

    peak, total, summed = lax.fori_loop(0, count // step, visit, init)
    return (
        (summed / total[..., None])
        .reshape(total_rows, kv_heads * query_group * HEAD_SIZE)
        .astype(jnp.bfloat16)
    )


def shards(
    activations,
    input_norm_gain,
    query_weight,
    key_weight,
    value_weight,
    output_weight,
    adapter_down_maps,
    query_up_maps,
    key_up_maps,
    value_up_maps,
    output_down_maps,
    output_up_maps,
    segment_index,
    segment_adapter,
):
    rows = activations.shape[0]
    features = activations.shape[1]
    head_split = lax.axis_size("uly")
    block_index = lax.axis_index("blk")
    head_index = lax.axis_index("uly")
    block_rows = rows * head_split
    block_start = block_index * block_rows
    own_start = block_start + head_index * rows
    hidden_width = ADAPTER_COUNT * ADAPTER_RANK
    tenant_index = tenant_rows(
        lax.dynamic_slice_in_dim(segment_index, own_start, rows), segment_adapter
    )
    normed_input = normalize(activations, input_norm_gain)
    lowered_rows = jnp.where(
        tenant_adapter_mask(tenant_index, 3 * hidden_width),
        jnp.dot(normed_input, adapter_down_maps, preferred_element_type=jnp.float32),
        0.0,
    ).astype(jnp.bfloat16)
    packed = jnp.concatenate([normed_input, lowered_rows], axis=1)
    piece = lax.all_gather(packed, "uly", axis=0, tiled=True)
    input_rows = piece[:, :features]
    rank_rows = piece[:, features:]
    query_part = jnp.dot(
        input_rows, query_weight, preferred_element_type=jnp.float32
    ) + adapter_scale * jnp.dot(
        rank_rows[:, :hidden_width], query_up_maps, preferred_element_type=jnp.float32
    )
    key_portion = jnp.dot(
        input_rows, key_weight, preferred_element_type=jnp.float32
    ) + adapter_scale * jnp.dot(
        rank_rows[:, hidden_width : 2 * hidden_width],
        key_up_maps,
        preferred_element_type=jnp.float32,
    )
    value_part = jnp.dot(
        input_rows, value_weight, preferred_element_type=jnp.float32
    ) + adapter_scale * jnp.dot(
        rank_rows[:, 2 * hidden_width :], value_up_maps, preferred_element_type=jnp.float32
    )
    projected = jnp.concatenate([query_part, key_portion, value_part], axis=1).astype(jnp.bfloat16)
    query_width = query_weight.shape[1]
    key_width = key_weight.shape[1]
    query_rows = projected[:, :query_width]
    key_matrix_rows = projected[:, query_width : query_width + key_width]
    value_matrix_rows = projected[:, query_width + key_width :]
    offsets = jnp.arange(block_rows, dtype=jnp.int32)
    query_pos = block_start + offsets
    mixed_heads = attend_local(
        query_rows, key_matrix_rows, value_matrix_rows, query_pos, segment_index
    )
    output_up_rows = output_up_maps.astype(jnp.float32)
    block_tenant = tenant_rows(
        lax.dynamic_slice_in_dim(segment_index, block_start, block_rows), segment_adapter
    )
    segment_block_mask = tenant_adapter_mask(block_tenant, hidden_width)
    lows_part = jnp.where(
        segment_block_mask,
        jnp.dot(mixed_heads, output_down_maps, preferred_element_type=jnp.float32),
        0.0,
    )
    summed = lax.psum_scatter(
        jnp.concatenate(
            [jnp.dot(mixed_heads, output_weight, preferred_element_type=jnp.float32), lows_part],
            axis=1,
        ).astype(jnp.bfloat16),
        "uly",
        scatter_dimension=0,
        tiled=True,
    ).astype(jnp.float32)
    main_entry = summed[:, :features]
    rank_rows = summed[:, features:]
    block_result = main_entry + adapter_scale * jnp.dot(
        rank_rows, output_up_rows, precision=lax.Precision.HIGHEST
    )
    return block_result.astype(jnp.bfloat16)


def solution(mesh):
    return jax.shard_map(
        shards,
        mesh=mesh,
        in_specs=(
            P(("blk", "uly"), None),
            P(),
            P(None, "uly"),
            P(None, "uly"),
            P(None, "uly"),
            P("uly", None),
            P(),
            P(None, "uly"),
            P(None, "uly"),
            P(None, "uly"),
            P("uly", None),
            P(),
            P(),
            P(),
        ),
        out_specs=P(("blk", "uly"), None),
        check_vma=False,
    )
```

profile of v0, /device:TPU:38, one launch (start us, length us, event | category | flops | bytes accessed | tf_op | source)
XLA Modules:
  0.0 531.6 jit_solution(7570707864134958057)
XLA Ops:
  12.8 96.3 %all-gather.4.cloned.1.call-done = bf16[768,4480]{1,0:T(8,128)(2,1)} async-done(((bf16[96,4480]{1,0:T(8,128)(2,1)}), bf16[768,4480]{1,0:T(8,128)(2,1)}) %all-gather.4.cloned.1.call-update) | async-done | bytes 6881296 | tf_op jit(solution)/shard_map/all_gather | solution.py:133
  139.8 8.8 %all-gather.8.cloned.1.call-done = bf16[12288,128]{1,0:T(8,128)(2,1)} async-done(((bf16[768,128]{1,0:T(8,128)(2,1)}), bf16[12288,128]{1,0:T(8,128)(2,1)}) %all-gather.8.cloned.1.call-update) | async-done | bytes 3145744 | tf_op jit(solution)/shard_map/all_gather | solution.py:49
  153.3 33.0 %all-gather.6.cloned.1.call-done = bf16[12288,128]{1,0:T(8,128)(2,1)} async-done(((bf16[768,128]{1,0:T(8,128)(2,1)}), bf16[12288,128]{1,0:T(8,128)(2,1)}) %all-gather.6.cloned.1.call-update) | async-done | bytes 3145744 | tf_op jit(solution)/shard_map/all_gather | solution.py:48
  187.6 213.7 %while.18 = (s32[]{:T(128)}, f32[768,1,4]{0,2,1:T(4,128)S(1)}, f32[768,1,4]{0,2,1:T(4,128)S(1)}, f32[768,1,4,128]{0,3,2,1:T(8,128)}, s32[]{:T(128)}, /*index=5*/...) while((s32[]{:T(128)}, f32[768,1,4]{0,2,1:T(4,128)S(1)}, ...), condition=%wide.region_8.9_spmd.clone, body=%wide.region_3.8_spmd.clone.sunk | while | flops 824584448 | bytes 24864092 | solution.py:90
  206.7 8.7 %conditional.3 = ((f32[768,1,4]{0,2,1:T(4,128)S(1)}, f32[768,1,4]{0,2,1:T(4,128)S(1)}, f32[768,1,4,128]{0,3,2,1:T(8,128)})) conditional(s32[]{:T(128)} %convert_element_type.58, (f32[768,1,4]{0,2,1:T(4,128)S(1)}, f32[768,1,4]{0,2,1:T(4,128)S(1)}, f32[768,1,4,128]{0,3,2,1:T(8,128)}) %tuple.48, (s32[]{:T(128)}, s32[]{:T(128)}, s32[12288]{0:T(1024)S(1)}, ...), branch_computations={%region_4.4_spmd, %region_5.7_spmd} | conditional | flops 824584448 | bytes 24860758 | solution.py:88
  215.9 8.7 %conditional.3 = ((f32[768,1,4]{0,2,1:T(4,128)S(1)}, f32[768,1,4]{0,2,1:T(4,128)S(1)}, f32[768,1,4,128]{0,3,2,1:T(8,128)})) conditional(s32[]{:T(128)} %convert_element_type.58, (f32[768,1,4]{0,2,1:T(4,128)S(1)}, f32[768,1,4]{0,2,1:T(4,128)S(1)}, f32[768,1,4,128]{0,3,2,1:T(8,128)}) %tuple.48, (s32[]{:T(128)}, s32[]{:T(128)}, s32[12288]{0:T(1024)S(1)}, ...), branch_computations={%region_4.4_spmd, %region_5.7_spmd} | conditional | flops 824584448 | bytes 24860758 | solution.py:88
  225.2 8.7 %conditional.3 = ((f32[768,1,4]{0,2,1:T(4,128)S(1)}, f32[768,1,4]{0,2,1:T(4,128)S(1)}, f32[768,1,4,128]{0,3,2,1:T(8,128)})) conditional(s32[]{:T(128)} %convert_element_type.58, (f32[768,1,4]{0,2,1:T(4,128)S(1)}, f32[768,1,4]{0,2,1:T(4,128)S(1)}, f32[768,1,4,128]{0,3,2,1:T(8,128)}) %tuple.48, (s32[]{:T(128)}, s32[]{:T(128)}, s32[12288]{0:T(1024)S(1)}, ...), branch_computations={%region_4.4_spmd, %region_5.7_spmd} | conditional | flops 824584448 | bytes 24860758 | solution.py:88
  234.5 8.7 %conditional.3 = ((f32[768,1,4]{0,2,1:T(4,128)S(1)}, f32[768,1,4]{0,2,1:T(4,128)S(1)}, f32[768,1,4,128]{0,3,2,1:T(8,128)})) conditional(s32[]{:T(128)} %convert_element_type.58, (f32[768,1,4]{0,2,1:T(4,128)S(1)}, f32[768,1,4]{0,2,1:T(4,128)S(1)}, f32[768,1,4,128]{0,3,2,1:T(8,128)}) %tuple.48, (s32[]{:T(128)}, s32[]{:T(128)}, s32[12288]{0:T(1024)S(1)}, ...), branch_computations={%region_4.4_spmd, %region_5.7_spmd} | conditional | flops 824584448 | bytes 24860758 | solution.py:88
  243.7 8.7 %conditional.3 = ((f32[768,1,4]{0,2,1:T(4,128)S(1)}, f32[768,1,4]{0,2,1:T(4,128)S(1)}, f32[768,1,4,128]{0,3,2,1:T(8,128)})) conditional(s32[]{:T(128)} %convert_element_type.58, (f32[768,1,4]{0,2,1:T(4,128)S(1)}, f32[768,1,4]{0,2,1:T(4,128)S(1)}, f32[768,1,4,128]{0,3,2,1:T(8,128)}) %tuple.48, (s32[]{:T(128)}, s32[]{:T(128)}, s32[12288]{0:T(1024)S(1)}, ...), branch_computations={%region_4.4_spmd, %region_5.7_spmd} | conditional | flops 824584448 | bytes 24860758 | solution.py:88
  253.0 8.7 %conditional.3 = ((f32[768,1,4]{0,2,1:T(4,128)S(1)}, f32[768,1,4]{0,2,1:T(4,128)S(1)}, f32[768,1,4,128]{0,3,2,1:T(8,128)})) conditional(s32[]{:T(128)} %convert_element_type.58, (f32[768,1,4]{0,2,1:T(4,128)S(1)}, f32[768,1,4]{0,2,1:T(4,128)S(1)}, f32[768,1,4,128]{0,3,2,1:T(8,128)}) %tuple.48, (s32[]{:T(128)}, s32[]{:T(128)}, s32[12288]{0:T(1024)S(1)}, ...), branch_computations={%region_4.4_spmd, %region_5.7_spmd} | conditional | flops 824584448 | bytes 24860758 | solution.py:88
  262.3 8.7 %conditional.3 = ((f32[768,1,4]{0,2,1:T(4,128)S(1)}, f32[768,1,4]{0,2,1:T(4,128)S(1)}, f32[768,1,4,128]{0,3,2,1:T(8,128)})) conditional(s32[]{:T(128)} %convert_element_type.58, (f32[768,1,4]{0,2,1:T(4,128)S(1)}, f32[768,1,4]{0,2,1:T(4,128)S(1)}, f32[768,1,4,128]{0,3,2,1:T(8,128)}) %tuple.48, (s32[]{:T(128)}, s32[]{:T(128)}, s32[12288]{0:T(1024)S(1)}, ...), branch_computations={%region_4.4_spmd, %region_5.7_spmd} | conditional | flops 824584448 | bytes 24860758 | solution.py:88
  271.5 8.7 %conditional.3 = ((f32[768,1,4]{0,2,1:T(4,128)S(1)}, f32[768,1,4]{0,2,1:T(4,128)S(1)}, f32[768,1,4,128]{0,3,2,1:T(8,128)})) conditional(s32[]{:T(128)} %convert_element_type.58, (f32[768,1,4]{0,2,1:T(4,128)S(1)}, f32[768,1,4]{0,2,1:T(4,128)S(1)}, f32[768,1,4,128]{0,3,2,1:T(8,128)}) %tuple.48, (s32[]{:T(128)}, s32[]{:T(128)}, s32[12288]{0:T(1024)S(1)}, ...), branch_computations={%region_4.4_spmd, %region_5.7_spmd} | conditional | flops 824584448 | bytes 24860758 | solution.py:88
  280.8 8.7 %conditional.3 = ((f32[768,1,4]{0,2,1:T(4,128)S(1)}, f32[768,1,4]{0,2,1:T(4,128)S(1)}, f32[768,1,4,128]{0,3,2,1:T(8,128)})) conditional(s32[]{:T(128)} %convert_element_type.58, (f32[768,1,4]{0,2,1:T(4,128)S(1)}, f32[768,1,4]{0,2,1:T(4,128)S(1)}, f32[768,1,4,128]{0,3,2,1:T(8,128)}) %tuple.48, (s32[]{:T(128)}, s32[]{:T(128)}, s32[12288]{0:T(1024)S(1)}, ...), branch_computations={%region_4.4_spmd, %region_5.7_spmd} | conditional | flops 824584448 | bytes 24860758 | solution.py:88
  290.0 8.7 %conditional.3 = ((f32[768,1,4]{0,2,1:T(4,128)S(1)}, f32[768,1,4]{0,2,1:T(4,128)S(1)}, f32[768,1,4,128]{0,3,2,1:T(8,128)})) conditional(s32[]{:T(128)} %convert_element_type.58, (f32[768,1,4]{0,2,1:T(4,128)S(1)}, f32[768,1,4]{0,2,1:T(4,128)S(1)}, f32[768,1,4,128]{0,3,2,1:T(8,128)}) %tuple.48, (s32[]{:T(128)}, s32[]{:T(128)}, s32[12288]{0:T(1024)S(1)}, ...), branch_computations={%region_4.4_spmd, %region_5.7_spmd} | conditional | flops 824584448 | bytes 24860758 | solution.py:88
  299.3 8.7 %conditional.3 = ((f32[768,1,4]{0,2,1:T(4,128)S(1)}, f32[768,1,4]{0,2,1:T(4,128)S(1)}, f32[768,1,4,128]{0,3,2,1:T(8,128)})) conditional(s32[]{:T(128)} %convert_element_type.58, (f32[768,1,4]{0,2,1:T(4,128)S(1)}, f32[768,1,4]{0,2,1:T(4,128)S(1)}, f32[768,1,4,128]{0,3,2,1:T(8,128)}) %tuple.48, (s32[]{:T(128)}, s32[]{:T(128)}, s32[12288]{0:T(1024)S(1)}, ...), branch_computations={%region_4.4_spmd, %region_5.7_spmd} | conditional | flops 824584448 | bytes 24860758 | solution.py:88
  308.6 8.7 %conditional.3 = ((f32[768,1,4]{0,2,1:T(4,128)S(1)}, f32[768,1,4]{0,2,1:T(4,128)S(1)}, f32[768,1,4,128]{0,3,2,1:T(8,128)})) conditional(s32[]{:T(128)} %convert_element_type.58, (f32[768,1,4]{0,2,1:T(4,128)S(1)}, f32[768,1,4]{0,2,1:T(4,128)S(1)}, f32[768,1,4,128]{0,3,2,1:T(8,128)}) %tuple.48, (s32[]{:T(128)}, s32[]{:T(128)}, s32[12288]{0:T(1024)S(1)}, ...), branch_computations={%region_4.4_spmd, %region_5.7_spmd} | conditional | flops 824584448 | bytes 24860758 | solution.py:88
  317.8 8.7 %conditional.3 = ((f32[768,1,4]{0,2,1:T(4,128)S(1)}, f32[768,1,4]{0,2,1:T(4,128)S(1)}, f32[768,1,4,128]{0,3,2,1:T(8,128)})) conditional(s32[]{:T(128)} %convert_element_type.58, (f32[768,1,4]{0,2,1:T(4,128)S(1)}, f32[768,1,4]{0,2,1:T(4,128)S(1)}, f32[768,1,4,128]{0,3,2,1:T(8,128)}) %tuple.48, (s32[]{:T(128)}, s32[]{:T(128)}, s32[12288]{0:T(1024)S(1)}, ...), branch_computations={%region_4.4_spmd, %region_5.7_spmd} | conditional | flops 824584448 | bytes 24860758 | solution.py:88
  327.1 8.7 %conditional.3 = ((f32[768,1,4]{0,2,1:T(4,128)S(1)}, f32[768,1,4]{0,2,1:T(4,128)S(1)}, f32[768,1,4,128]{0,3,2,1:T(8,128)})) conditional(s32[]{:T(128)} %convert_element_type.58, (f32[768,1,4]{0,2,1:T(4,128)S(1)}, f32[768,1,4]{0,2,1:T(4,128)S(1)}, f32[768,1,4,128]{0,3,2,1:T(8,128)}) %tuple.48, (s32[]{:T(128)}, s32[]{:T(128)}, s32[12288]{0:T(1024)S(1)}, ...), branch_computations={%region_4.4_spmd, %region_5.7_spmd} | conditional | flops 824584448 | bytes 24860758 | solution.py:88
  336.4 8.7 %conditional.3 = ((f32[768,1,4]{0,2,1:T(4,128)S(1)}, f32[768,1,4]{0,2,1:T(4,128)S(1)}, f32[768,1,4,128]{0,3,2,1:T(8,128)})) conditional(s32[]{:T(128)} %convert_element_type.58, (f32[768,1,4]{0,2,1:T(4,128)S(1)}, f32[768,1,4]{0,2,1:T(4,128)S(1)}, f32[768,1,4,128]{0,3,2,1:T(8,128)}) %tuple.48, (s32[]{:T(128)}, s32[]{:T(128)}, s32[12288]{0:T(1024)S(1)}, ...), branch_computations={%region_4.4_spmd, %region_5.7_spmd} | conditional | flops 824584448 | bytes 24860758 | solution.py:88
  345.6 8.7 %conditional.3 = ((f32[768,1,4]{0,2,1:T(4,128)S(1)}, f32[768,1,4]{0,2,1:T(4,128)S(1)}, f32[768,1,4,128]{0,3,2,1:T(8,128)})) conditional(s32[]{:T(128)} %convert_element_type.58, (f32[768,1,4]{0,2,1:T(4,128)S(1)}, f32[768,1,4]{0,2,1:T(4,128)S(1)}, f32[768,1,4,128]{0,3,2,1:T(8,128)}) %tuple.48, (s32[]{:T(128)}, s32[]{:T(128)}, s32[12288]{0:T(1024)S(1)}, ...), branch_computations={%region_4.4_spmd, %region_5.7_spmd} | conditional | flops 824584448 | bytes 24860758 | solution.py:88
  354.9 8.7 %conditional.3 = ((f32[768,1,4]{0,2,1:T(4,128)S(1)}, f32[768,1,4]{0,2,1:T(4,128)S(1)}, f32[768,1,4,128]{0,3,2,1:T(8,128)})) conditional(s32[]{:T(128)} %convert_element_type.58, (f32[768,1,4]{0,2,1:T(4,128)S(1)}, f32[768,1,4]{0,2,1:T(4,128)S(1)}, f32[768,1,4,128]{0,3,2,1:T(8,128)}) %tuple.48, (s32[]{:T(128)}, s32[]{:T(128)}, s32[12288]{0:T(1024)S(1)}, ...), branch_computations={%region_4.4_spmd, %region_5.7_spmd} | conditional | flops 824584448 | bytes 24860758 | solution.py:88
  364.2 8.7 %conditional.3 = ((f32[768,1,4]{0,2,1:T(4,128)S(1)}, f32[768,1,4]{0,2,1:T(4,128)S(1)}, f32[768,1,4,128]{0,3,2,1:T(8,128)})) conditional(s32[]{:T(128)} %convert_element_type.58, (f32[768,1,4]{0,2,1:T(4,128)S(1)}, f32[768,1,4]{0,2,1:T(4,128)S(1)}, f32[768,1,4,128]{0,3,2,1:T(8,128)}) %tuple.48, (s32[]{:T(128)}, s32[]{:T(128)}, s32[12288]{0:T(1024)S(1)}, ...), branch_computations={%region_4.4_spmd, %region_5.7_spmd} | conditional | flops 824584448 | bytes 24860758 | solution.py:88
  382.7 8.7 %conditional.3 = ((f32[768,1,4]{0,2,1:T(4,128)S(1)}, f32[768,1,4]{0,2,1:T(4,128)S(1)}, f32[768,1,4,128]{0,3,2,1:T(8,128)})) conditional(s32[]{:T(128)} %convert_element_type.58, (f32[768,1,4]{0,2,1:T(4,128)S(1)}, f32[768,1,4]{0,2,1:T(4,128)S(1)}, f32[768,1,4,128]{0,3,2,1:T(8,128)}) %tuple.48, (s32[]{:T(128)}, s32[]{:T(128)}, s32[12288]{0:T(1024)S(1)}, ...), branch_computations={%region_4.4_spmd, %region_5.7_spmd} | conditional | flops 824584448 | bytes 24860758 | solution.py:88
  412.4 109.9 %reduce-scatter.2.cloned.1.call-done = bf16[96,4224]{1,0:T(8,128)(2,1)} async-done(((bf16[768,4224]{1,0:T(8,128)(2,1)}), bf16[96,4224]{1,0:T(8,128)(2,1)}) %reduce-scatter.2.cloned.1.call-update) | async-done | bytes 811024 | tf_op jit(solution)/shard_map/reduce_scatter | solution.py:174
  (312 shorter events, 289.2 us)
Async XLA Ops:
  6.5 4.5 copy-start
  6.5 102.5 %all-gather.4.cloned.1.call-start = ((), (), s32[]{:S(2)}) async-start(), calls=%async_computation.1 | async-start | bytes 7741440 | tf_op jit(solution)/shard_map/all_gather | solution.py:133
  12.7 101.2 %copy-start.3 = (bf16[128,128]{1,0:T(8,128)(2,1)S(1)}, bf16[128,128]{1,0:T(8,128)(2,1)}, u32[]{:S(2)}) copy-start(bf16[128,128]{1,0:T(8,128)(2,1)} %param.27) | copy-start | bytes 98308
  12.7 135.9 %all-gather.8.cloned.1.call-start = ((), (), s32[]{:S(2)}) async-start(), calls=%async_computation.3 | async-start | bytes 3342336 | tf_op jit(solution)/shard_map/all_gather | solution.py:49
  115.7 4.9 copy-start.4
  115.7 7.0 %copy-start.1 = (s32[12288]{0:T(1024)S(1)}, s32[12288]{0:T(1024)}, u32[]{:S(2)}) copy-start(s32[12288]{0:T(1024)} %param.30) | copy-start | bytes 147460
  115.7 70.5 %all-gather.6.cloned.1.call-start = ((), (), s32[]{:S(2)}) async-start(), calls=%async_computation.2 | async-start | bytes 3342336 | tf_op jit(solution)/shard_map/all_gather | solution.py:48
  120.6 6.7 %copy-start.5 = (s32[4]{0:T(128)S(1)}, s32[4]{0:T(128)}, u32[]{:S(2)}) copy-start(s32[4]{0:T(128)} %param.31) | copy-start | bytes 52
  122.5 399.8 %reduce-scatter.2.cloned.1.call-start = ((), (), s32[]{:S(2)}) async-start(), calls=%async_computation.4 | async-start | bytes 7299072 | tf_op jit(solution)/shard_map/reduce_scatter | solution.py:174
  128.0 7.2 %copy-start.2 = (bf16[128,512]{1,0:T(8,128)(2,1)S(1)}, bf16[128,512]{1,0:T(8,128)(2,1)}, u32[]{:S(2)}) copy-start(bf16[128,512]{1,0:T(8,128)(2,1)} %param.25) | copy-start | bytes 393220
  402.8 6.0 %copy-start.6 = (bf16[512,128]{1,0:T(8,128)(2,1)S(1)}, bf16[512,128]{1,0:T(8,128)(2,1)}, u32[]{:S(2)}) copy-start(bf16[512,128]{1,0:T(8,128)(2,1)} %param.28) | copy-start | bytes 393220
Sparse Core Ops, SparseCore 0:
  12.8 96.1 all-gather.3
  115.8 32.7 all-gather.7
  150.3 35.9 all-gather.5
  412.6 109.7 reduce-scatter.1
where the time goes:
time: 535 us; the launch traced here: 532 us
  waiting for transfers between devices  248 us (46%)
  matrix products  188 us (35%)
  other arithmetic  50.7 us (9%)
  loops' own time  15.8 us (3%)
  local copies, waits for them, and re-layouts  15.6 us (3%)
  between operations  13.3 us (2%)
    reduce_scatter x1, waiting for transfers between devices, shards(): lax.psum_scatter(jnp.concatenate([jnp.dot(mixed_heads, output_weight, pre...  110 us
    dot_general x23, matrix products, compute(): jnp.einsum('rkgn,nkd->rkgd', weights.astype(jnp.bfloat16), value_block, p...  99.4 us
    all_gather x1, waiting for transfers between devices, shards(): piece = lax.all_gather(packed, 'uly', axis=0, tiled=True)  96.3 us
    dot_general x23, matrix products, compute(): jnp.einsum('rkgd,nkd->rkgn', query_matrix, key_block, preferred_element_t...  56 us
    all_gather x1, waiting for transfers between devices, attend_local(): key_piece = lax.all_gather(key_matrix_rows, 'blk', axis=0, tiled=True)  33 us
    reduce_sum x23, other arithmetic, compute(): total = total * decay + jnp.sum(weights, axis=3)  31 us
    another operation x1, loops' own time, attend_local(): peak, total, summed = lax.fori_loop(0, count // step, visit, init)  14.5 us
  transfers between devices with their start and end apart: 4, of which 4 were waited for; matrix products, arithmetic and copies ran while one was open for 5% of the time, Pallas kernels for 0%

commit v1 on v0

v1 whole, which is shorter than its diff:
```python
import functools
import math

import jax
import jax.numpy as jnp
from jax import lax
from jax.experimental import pallas as pl
from jax.experimental.pallas import tpu as pltpu
from jax.sharding import PartitionSpec as P

HEAD_SIZE = 128
ADAPTER_RANK = 16
ADAPTER_COUNT = 8
GROUP = 4
PIECE = 96
HALF = 384
BLOCK = 768
BLOCKS = 16
EPS_NORM = 1e-05
ADAPTER_SCALE = 2.0
MASKED = -1e30
LEAST = -1e20
EXP2_SCALE = math.log2(math.e) / math.sqrt(HEAD_SIZE)
MIB = 2**20

INFO = 24


def pos_of(info, bases, width, axis):
    shape = (width * len(bases), 1) if axis == 0 else (1, width * len(bases))
    index = lax.broadcasted_iota(jnp.int32, shape, axis)
    pos = index + info[bases[0]]
    for i, base in enumerate(bases[1:], 1):
        pos = jnp.where(index >= i * width, index + (info[base] - i * width), pos)
    return pos


def start_of(info, pos):
    start = jnp.zeros_like(pos)
    for s in range(8, 11):
        start = jnp.where(pos >= info[s], info[s], start)
    return start


def tenant_of(info, pos):
    tenant = jnp.zeros_like(pos) + info[11]
    for s in range(3):
        tenant = jnp.where(pos >= info[8 + s], info[12 + s], tenant)
    return tenant


def keep_columns(info, bases, columns):
    tenant = tenant_of(info, pos_of(info, bases, PIECE, 0))
    column = lax.broadcasted_iota(jnp.int32, (len(bases) * PIECE, columns), 1)
    return (column // ADAPTER_RANK) % ADAPTER_COUNT == tenant


def project_kernel(info, *refs, bases, parts):
    rows = refs[:parts]
    wq, wk, wv, down, q_up, k_up, v_up, q_out, kv_out, acc = refs[parts:]
    step = pl.program_id(0)
    x = jnp.concatenate([r[...] for r in rows], axis=0)
    nq, nk = wq.shape[1], wk.shape[1]
    spans = ((0, nq, wq), (nq, nk, wk), (nq + nk, nk, wv), (nq + 2 * nk, down.shape[1], down))

    @pl.when(step == 0)
    def _():
        for at, width, w in spans:
            acc[:, at : at + width] = jnp.dot(x, w[...], preferred_element_type=jnp.float32)

    @pl.when(step > 0)
    def _():
        for at, width, w in spans:
            acc[:, at : at + width] += jnp.dot(x, w[...], preferred_element_type=jnp.float32)

    @pl.when(step == pl.num_programs(0) - 1)
    def _():
        hidden = ADAPTER_COUNT * ADAPTER_RANK
        low = acc[:, nq + 2 * nk :]
        low = jnp.where(keep_columns(info, bases, 3 * hidden), low, 0.0).astype(jnp.bfloat16)

        def with_adapter(at, width, i, up):
            return (
                acc[:, at : at + width]
                + ADAPTER_SCALE
                * jnp.dot(
                    low[:, i * hidden : (i + 1) * hidden],
                    up[...],
                    preferred_element_type=jnp.float32,
                )
            ).astype(jnp.bfloat16)

        q_out[...] = with_adapter(0, nq, 0, q_up)
        kv_out[:, :nk] = with_adapter(nq, nk, 1, k_up)
        kv_out[:, nk:] = with_adapter(nq + nk, nk, 2, v_up)


def project(info, rows, bases, wq, wk, wv, down, q_up, k_up, v_up):
    depth, nq, nk = wq.shape[0], wq.shape[1], wk.shape[1]
    count = sum(r.shape[0] for r in rows)
    chunk = 1024
    along = lambda a: pl.BlockSpec((a.shape[0], chunk), lambda i, s: (0, i))
    down_ = lambda a: pl.BlockSpec((chunk, a.shape[1]), lambda i, s: (i, 0))
    whole = lambda a: pl.BlockSpec(a.shape, lambda i, s: (0, 0))
    wide = nq + 2 * nk + down.shape[1]
    return pl.pallas_call(
        functools.partial(project_kernel, bases=bases, parts=len(rows)),
        out_shape=(
            jax.ShapeDtypeStruct((count, nq), jnp.bfloat16),
            jax.ShapeDtypeStruct((count, 2 * nk), jnp.bfloat16),
        ),
        grid_spec=pltpu.PrefetchScalarGridSpec(
            num_scalar_prefetch=1,
            grid=(depth // chunk,),
            in_specs=[along(r) for r in rows]
            + [down_(w) for w in (wq, wk, wv, down)]
            + [whole(u) for u in (q_up, k_up, v_up)],
            out_specs=(
                pl.BlockSpec((count, nq), lambda i, s: (0, 0)),
                pl.BlockSpec((count, 2 * nk), lambda i, s: (0, 0)),
            ),
            scratch_shapes=[pltpu.VMEM((count, wide), jnp.float32)],
        ),
        compiler_params=pltpu.CompilerParams(vmem_limit_bytes=48 * MIB),
        cost_estimate=pl.CostEstimate(
            flops=2 * count * depth * wide,
            bytes_accessed=2 * depth * (wide + count),
            transcendentals=0,
        ),
    )(info, *rows, wq, wk, wv, down, q_up, k_up, v_up)


def attend_kernel(info, q1, q2, kv1, kv2, out, kv, sem, qt, acc, peak, held, held_peak, *, own, tile, width):
    copies = []
    for part, pieces in ((kv1, ((0, 15), (1, 16), (2, 17), (3, 19))), (kv2, ((0, 18), (1, 20), (2, 21), (3, 22)))):
        for i, place in pieces:
            to = pl.ds(pl.multiple_of(info[place] * PIECE, PIECE), PIECE)
            if place < 19:
                copies.append((part.at[:, :, :, i], kv.at[:, :, :, to]))
            else:
                for z in range(2):
                    copies.append((part.at[:, z, :, i], kv.at[:, 1 - z, :, to]))
    started = []
    for n, (source, target) in enumerate(copies):
        started.append(pltpu.make_async_copy(source, target, sem.at[n]))
        started[-1].start()
    if own:
        groups = ((q1, 0, 0, 3), (q2, 0, 3, 1))
        bases = (0, 1, 2, 3)
    else:
        groups = ((q1, 3, 0, 1), (q2, 1, 1, 3))
        bases = (4, 5, 6, 7)
    q = jnp.concatenate([r[a * PIECE : (a + n) * PIECE] for r, a, _, n in groups], axis=0)
    for h in range(GROUP):
        qt[:, h * HALF : (h + 1) * HALF] = q[:, h * HEAD_SIZE : (h + 1) * HEAD_SIZE].T
    total = GROUP * HALF
    peak[...] = jnp.full((1, total), LEAST, jnp.float32)
    acc[...] = jnp.zeros((HEAD_SIZE + 8, total), jnp.float32)
    pos = pos_of(info, bases, PIECE, 1)
    low = start_of(info, pos)
    pos = jnp.concatenate([pos] * GROUP, axis=1)
    low = jnp.concatenate([low] * GROUP, axis=1)
    first = info[bases[0]]
    for b in bases[1:]:
        first = jnp.minimum(first, info[b])
    last = first + (HALF - 1)
    n0 = start_of(info, first) // tile
    n3 = last // tile + 1
    m1 = jnp.clip((start_of(info, last) + tile - 1) // tile, n0, n3)
    m2 = jnp.clip(first // tile, m1, n3)
    ahead = m1 - n0
    for c in started:
        c.wait()

    def of_tile(j, at):
        return kv[j // 4, (j // 2) % 2, j % 2, :, at : at + HEAD_SIZE]

    def step(now, later, masked):
        if later is not None:
            keys = of_tile(later, 0)
        if now is not None:
            values = jnp.concatenate(
                [of_tile(now, HEAD_SIZE).T, jnp.ones((8, tile), jnp.bfloat16)], axis=0
            )
        for c in range(0, total, width):
            at = slice(c, c + width)
            if now is not None:
                old = peak[:, at]
                fresh = jnp.maximum(old, held_peak[:, at])
                weights = jnp.exp2((held[:, at] - fresh) * EXP2_SCALE).astype(jnp.bfloat16)
                decay = jnp.exp2((old - fresh) * EXP2_SCALE)
                peak[:, at] = fresh
            if later is not None:
                scores = jnp.dot(keys, qt[:, at], preferred_element_type=jnp.float32)
                if masked:
                    key_pos = later * tile + lax.broadcasted_iota(jnp.int32, (tile, width), 0)
                    allowed = (key_pos <= pos[:, at]) & (key_pos >= low[:, at])
                    scores = jnp.where(allowed, scores, MASKED)
                held[:, at] = scores
                held_peak[:, at] = jnp.max(scores, axis=0, keepdims=True)
            if now is not None:
                acc[:, at] = acc[:, at] * decay + jnp.dot(
                    values, weights, preferred_element_type=jnp.float32
                )

    def masked_tile(i):
        return jnp.where(i < ahead, n0 + i, m2 + i - ahead)

    def masked_step(i, now):
        step(now, masked_tile(i), True)
        return masked_tile(i)

    def plain_step(j, now):
        step(now, j, False)
        return j

    step(None, masked_tile(0), True)
    now = lax.fori_loop(1, ahead + n3 - m2, masked_step, masked_tile(0))
    now = lax.fori_loop(m1, m2, plain_step, now)
    step(now, None, False)
    for h in range(GROUP):
        at = slice(h * HALF, (h + 1) * HALF)
        mixed = acc[:HEAD_SIZE, at] / acc[HEAD_SIZE : HEAD_SIZE + 1, at]
        out[:, h * HEAD_SIZE : (h + 1) * HEAD_SIZE] = mixed.T.astype(jnp.bfloat16)


def attend(info, q1, q2, kv1, kv2, own):
    total = GROUP * HALF
    tile, width = BLOCK, 512
    flat = lambda a: pl.BlockSpec(a.shape, lambda i, s: (0, 0))
    anywhere = pl.BlockSpec(memory_space=pl.ANY)
    return pl.pallas_call(
        functools.partial(attend_kernel, own=own, tile=tile, width=width),
        out_shape=jax.ShapeDtypeStruct((HALF, GROUP * HEAD_SIZE), jnp.bfloat16),
        grid_spec=pltpu.PrefetchScalarGridSpec(
            num_scalar_prefetch=1,
            grid=(1,),
            in_specs=[flat(q1), flat(q2), anywhere, anywhere],
            out_specs=pl.BlockSpec((HALF, GROUP * HEAD_SIZE), lambda i, s: (0, 0)),
            scratch_shapes=[
                pltpu.VMEM((4, 2, 2, BLOCK, 2 * HEAD_SIZE), jnp.bfloat16),
                pltpu.SemaphoreType.DMA((12,)),
                pltpu.VMEM((HEAD_SIZE, total), jnp.bfloat16),
                pltpu.VMEM((HEAD_SIZE + 8, total), jnp.float32),
                pltpu.VMEM((1, total), jnp.float32),
                pltpu.VMEM((tile, total), jnp.float32),
                pltpu.VMEM((1, total), jnp.float32),
            ],
        ),
        compiler_params=pltpu.CompilerParams(vmem_limit_bytes=48 * MIB),
        cost_estimate=pl.CostEstimate(
            flops=2 * 2 * total * BLOCKS * BLOCK * HEAD_SIZE,
            bytes_accessed=8 * MIB,
            transcendentals=total * BLOCKS * BLOCK,
        ),
    )(info, q1, q2, kv1, kv2)


def output_kernel(info, mixed, weight, down, up, *rest, bases):
    *outs, high, rest_low = rest

    @pl.when(pl.program_id(0) == 0)
    def _():
        lows = jnp.dot(mixed[...], down[...], preferred_element_type=jnp.float32)
        lows = jnp.where(keep_columns(info, bases, lows.shape[1]), ADAPTER_SCALE * lows, 0.0)
        top = lows.astype(jnp.bfloat16)
        high[...] = top
        rest_low[...] = (lows - top.astype(jnp.float32)).astype(jnp.bfloat16)

    result = jnp.dot(mixed[...], weight[...], preferred_element_type=jnp.float32)
    result += jnp.dot(high[...], up[...], preferred_element_type=jnp.float32)
    result += jnp.dot(rest_low[...], up[...], preferred_element_type=jnp.float32)
    result = result.astype(jnp.bfloat16)
    for i, out in enumerate(outs):
        out[...] = result[i * PIECE : (i + 1) * PIECE]


def output(info, mixed, weight, down, up, bases):
    features = weight.shape[1]
    chunk = 512
    whole = lambda a: pl.BlockSpec(a.shape, lambda i, s: (0, 0))
    across = lambda n: pl.BlockSpec((n, chunk), lambda i, s: (0, i))
    return pl.pallas_call(
        functools.partial(output_kernel, bases=bases),
        out_shape=(jax.ShapeDtypeStruct((PIECE, features), jnp.bfloat16),) * 4,
        grid_spec=pltpu.PrefetchScalarGridSpec(
            num_scalar_prefetch=1,
            grid=(features // chunk,),
            in_specs=[whole(mixed), across(weight.shape[0]), whole(down), across(up.shape[0])],
            out_specs=(across(PIECE),) * 4,
            scratch_shapes=[pltpu.VMEM((HALF, down.shape[1]), jnp.bfloat16)] * 2,
        ),
        compiler_params=pltpu.CompilerParams(vmem_limit_bytes=48 * MIB),
        cost_estimate=pl.CostEstimate(
            flops=2 * HALF * (weight.shape[0] + 2 * up.shape[0]) * features,
            bytes_accessed=2 * features * (weight.shape[0] + up.shape[0] + HALF),
            transcendentals=0,
        ),
    )(info, mixed, weight, down, up)


def normalize(activations, input_norm_gain):
    values = activations.astype(jnp.float32)
    power = jnp.mean(values * values, axis=1, keepdims=True)
    return (values * lax.rsqrt(power + EPS_NORM) * input_norm_gain[None, :]).astype(jnp.bfloat16)


def along_y(rows, hop):
    return lax.ppermute(
        rows, "uly", [(z * 4 + y, z * 4 + (y + hop) % 4) for z in range(2) for y in range(4)]
    )


def across_z(rows):
    pairs = [(b * 8 + u, (b ^ 2) * 8 + (u ^ 4)) for b in range(16) for u in range(8)]
    return lax.ppermute(rows, ("blk", "uly"), pairs)


def plan(segment_index, segment_adapter):
    block, head = lax.axis_index("blk"), lax.axis_index("uly")
    z, y = head // 4, head % 4
    ys = [y, (y + 3) % 4, (y + 1) % 4, (y + 2) % 4]
    here = [z * 4 + p for p in ys]
    there = [(1 - z) * 4 + p for p in ys]
    firsts = [block * BLOCK + p * PIECE for p in here]
    firsts += [(block ^ 2) * BLOCK + p * PIECE for p in there]
    ends = jnp.sum(
        segment_index[None, :] < jnp.arange(1, 4, dtype=jnp.int32)[:, None], axis=1, dtype=jnp.int32
    )
    return jnp.concatenate(
        [
            jnp.stack(firsts).astype(jnp.int32),
            ends,
            segment_adapter,
            jnp.stack(here + there).astype(jnp.int32),
            jnp.zeros((INFO - 23,), jnp.int32),
        ]
    )


def added(*terms):
    return sum(t.astype(jnp.float32) for t in terms).astype(jnp.bfloat16)


def shards(
    activations,
    input_norm_gain,
    query_weight,
    key_weight,
    value_weight,
    output_weight,
    adapter_down_maps,
    query_up_maps,
    key_up_maps,
    value_up_maps,
    output_down_maps,
    output_up_maps,
    segment_index,
    segment_adapter,
):
    info = plan(segment_index, segment_adapter)
    weights = (
        query_weight,
        key_weight,
        value_weight,
        adapter_down_maps,
        query_up_maps,
        key_up_maps,
        value_up_maps,
    )
    mid = PIECE // 2
    own = normalize(activations, input_norm_gain)
    own_m, own_p, other = along_y(own, 1), along_y(own, -1), across_z(own)
    far_top, far_end = along_y(own_m[:mid], 1), along_y(own_p[mid:], -1)
    other_m, other_p = along_y(other, 1), along_y(other, -1)
    other_far = across_z(jnp.concatenate([far_top, far_end], axis=0))

    def gathered(kv):
        return lax.all_gather(kv, "blk", axis=0).reshape(4, 2, 2, 4, PIECE, 2 * HEAD_SIZE)

    q1, kv1 = project(info, [own, own_m, own_p, other], (0, 1, 2, 4), *weights)
    kv1 = gathered(kv1)
    q2, kv2 = project(
        info, [far_top, far_end, other_m, other_p, other_far], (3, 5, 6, 7), *weights
    )
    kv2 = gathered(kv2)

    out_weights = (output_weight, output_down_maps, output_up_maps)
    mixed = attend(info, q1, q2, kv1, kv2, False)
    b0, bm, bp, bf = output(info, mixed, *out_weights, (4, 5, 6, 7))
    for_far = across_z(bf)
    from_m, from_p = along_y(bp, 1), along_y(bm, -1)
    mixed = attend(info, q1, q2, kv1, kv2, True)
    a0, am, ap, af = output(info, mixed, *out_weights, (0, 1, 2, 3))
    for_other = across_z(added(b0, from_m, from_p))
    far = added(af, for_far)
    top, end = along_y(far[:mid], 1), along_y(far[mid:], -1)
    to_p = jnp.concatenate([added(ap[:mid], top), ap[mid:]], axis=0)
    to_m = jnp.concatenate([am[:mid], added(am[mid:], end)], axis=0)
    return added(a0, along_y(to_p, 1), along_y(to_m, -1), for_other)


def solution(mesh):
    return jax.shard_map(
        shards,
        mesh=mesh,
        in_specs=(
            P(("blk", "uly"), None),
            P(),
            P(None, "uly"),
            P(None, "uly"),
            P(None, "uly"),
            P("uly", None),
            P(),
            P(None, "uly"),
            P(None, "uly"),
            P(None, "uly"),
            P("uly", None),
            P(),
            P(),
            P(),
        ),
        out_specs=P(("blk", "uly"), None),
        check_vma=False,
    )
```

time: 535 us -> 237 us (0.44)
  matrix products: 188 us -> 0 us
  waiting for transfers between devices: 248 us -> 108 us
  Pallas kernels: 0 us -> 75.8 us
  other arithmetic: 50.7 us -> 6.17 us
  starting transfers between devices: 0.31 us -> 28.8 us
  loops' own time: 15.8 us -> 0 us
  local copies, waits for them, and re-layouts: 15.6 us -> 5.68 us
    dot_general x56 -> x0, matrix products: 188 us -> none  [the longest x23 99.4 us: compute(): jnp.einsum('rkgn,nkd->rkgd', weights.astype(jnp.bfloat16), value_block, p...]
    reduce_scatter x1 -> x0, waiting for transfers between devices: 110 us -> none  [shards(): lax.psum_scatter(jnp.concatenate([jnp.dot(mixed_heads, output_weight, pre...]
    all_gather x3 -> x2, waiting for transfers between devices: 138 us -> 34.1 us  [gathered(): lax.all_gather(kv, 'blk', axis=0).reshape(4, 2, 2, 4, PIECE, 2 * HEAD_SIZE)]
    pallas_call x0 -> x6, Pallas kernels: none -> 75.8 us  [the longest x2 41.1 us: attend(): pl.pallas_call(functools.partial(attend_kernel, own=own, tile=tile, width...]
    ppermute x0 -> x16, waiting for transfers between devices: none -> 74.1 us  [the longest x12 56.8 us: along_y(): lax.ppermute(rows, 'uly', [(z * 4 + y, z * 4 + (y + hop) % 4) for z in ra...]
    reduce_sum x25 -> x1, other arithmetic: 31.8 us -> 1.08 us  [plan(): jnp.sum(segment_index[None, :] < jnp.arange(1, 4, dtype=jnp.int32)[:, Non...]
    ppermute x0 -> x16, starting transfers between devices: none -> 28.7 us  [the longest x12 17 us: along_y(): lax.ppermute(rows, 'uly', [(z * 4 + y, z * 4 + (y + hop) % 4) for z in ra...]
    another operation x25 -> x0, loops' own time: 15.8 us -> none  [the longest x1 14.5 us: attend_local(): peak, total, summed = lax.fori_loop(0, count // step, visit, init)]
  transfers between devices with their start and end apart: 4 -> 18, of which waited for: 4 -> 15; matrix products, arithmetic and copies ran while one was open for 5% -> 1% of each run, Pallas kernels for 0% -> 17%
where the time goes in v1:
time: 237 us; the launch traced here: 238 us
  waiting for transfers between devices  108 us (46%)
  Pallas kernels  75.8 us (32%)
  starting transfers between devices  28.8 us (12%)
  between operations  13.6 us (6%)
  other arithmetic  6.17 us (3%)
  local copies, waits for them, and re-layouts  5.68 us (2%)
    ppermute x12, waiting for transfers between devices, along_y(): lax.ppermute(rows, 'uly', [(z * 4 + y, z * 4 + (y + hop) % 4) for z in ra...  56.8 us
    pallas_call x2, Pallas kernels, attend(): pl.pallas_call(functools.partial(attend_kernel, own=own, tile=tile, width...  41.1 us
    all_gather x2, waiting for transfers between devices, gathered(): lax.all_gather(kv, 'blk', axis=0).reshape(4, 2, 2, 4, PIECE, 2 * HEAD_SIZE)  34.1 us
    pallas_call x2, Pallas kernels, project(): pl.pallas_call(functools.partial(project_kernel, bases=bases, parts=len(r...  18.2 us
    ppermute x4, waiting for transfers between devices, across_z(): return lax.ppermute(rows, ('blk', 'uly'), pairs)  17.4 us
    ppermute x12, starting transfers between devices, along_y(): lax.ppermute(rows, 'uly', [(z * 4 + y, z * 4 + (y + hop) % 4) for z in ra...  17 us
    pallas_call x2, Pallas kernels, output(): pl.pallas_call(functools.partial(output_kernel, bases=bases), out_shape=(...  16.4 us
    ppermute x4, starting transfers between devices, across_z(): return lax.ppermute(rows, ('blk', 'uly'), pairs)  11.7 us
  transfers between devices with their start and end apart: 18, of which 15 were waited for; matrix products, arithmetic and copies ran while one was open for 1% of the time, Pallas kernels for 17%

profile of v1, /device:TPU:38, one launch (start us, length us, event | category | flops | bytes accessed | tf_op | source)
XLA Modules:
  0.0 238.3 jit_solution(6965227484260530415)
XLA Ops:
  9.5 2.0 collective-permute-start.2
  11.4 3.0 %collective-permute-start.1 = (bf16[96,4096]{1,0:T(8,128)(2,1)S(1)}, bf16[96,4096]{1,0:T(8,128)(2,1)S(1)}, u32[]{:S(2)}, u32[]{:S(2)}) collective-permute-start(bf16[96,4096]{1,0:T(8,128)(2,1)S(1)} %fusion.2.refs_0_), channel_id=1, source_target_pairs={{0,3},{1,0},{2,1},{3,2},{4,7},{5,4},{6,5},{7,6},{8,11},{9,8},{10,9... | collective-permute-start | bytes 2359304 | tf_op jit(solution)/shard_map/ppermute | solution.py:309
  15.7 13.4 %collective-permute-done.2.refs_3_ = bf16[96,4096]{1,0:T(8,128)(2,1)} collective-permute-done((bf16[96,4096]{1,0:T(8,128)(2,1)S(1)}, bf16[96,4096]{1,0:T(8,128)(2,1)}, u32[]{:S(2)}, u32[]{:S(2)}) %collective-permute-start.2) | collective-permute-done | bytes 786464 | tf_op jit(solution)/shard_map/ppermute | solution.py:316
  29.1 1.9 collective-permute-done.1.refs_2_
  31.0 3.4 %collective-permute-done.refs_1_ = bf16[96,4096]{1,0:T(8,128)(2,1)S(1)} collective-permute-done((bf16[96,4096]{1,0:T(8,128)(2,1)S(1)}, bf16[96,4096]{1,0:T(8,128)(2,1)S(1)}, u32[]{:S(2)}, u32[]{:S(2)}) %collective-permute-start) | collective-permute-done | bytes 786464 | tf_op jit(solution)/shard_map/ppermute | solution.py:309
  37.1 9.1 %shard_map.136 = (bf16[384,512]{1,0:T(8,128)(2,1)S(1)}, bf16[384,256]{1,0:T(8,128)(2,1)}) custom-call(s32[24]{0:T(128)S(1)} %concatenate.12.info, bf16[96,4096]{1,0:T(8,128)(2,1)S(1)} %fusion.2.refs_0_, bf16[96,4096]{1,0:T(8,128)(2,1)S(1)} %collective-permute-done.refs_1_, bf16[96,4096]{1,0:T(8,128)(2,1)S(1)} %collective-permute-done.1.refs_2_, ...), custom_call_target="tpu_custom_call" | custom-call | flops 3623878656 | bytes 12582912 | tf_op jit(solution)/shard_map/pallas_call | solution.py:106
  51.4 7.9 %collective-permute-done.4.refs_1_ = bf16[48,4096]{1,0:T(8,128)(2,1)S(1)} collective-permute-done((bf16[48,4096]{1,0:T(8,128)(2,1)S(1)}, bf16[48,4096]{1,0:T(8,128)(2,1)S(1)}, u32[]{:S(2)}, u32[]{:S(2)}) %collective-permute-start.4) | collective-permute-done | bytes 393248 | tf_op jit(solution)/shard_map/ppermute | solution.py:309
  61.4 12.1 %collective-permute-done.6.refs_3_ = bf16[96,4096]{1,0:T(8,128)(2,1)S(1)} collective-permute-done((bf16[96,4096]{1,0:T(8,128)(2,1)}, bf16[96,4096]{1,0:T(8,128)(2,1)S(1)}, u32[]{:S(2)}, u32[]{:S(2)}) %collective-permute-start.6) | collective-permute-done | bytes 786464 | tf_op jit(solution)/shard_map/ppermute | solution.py:309
  75.3 9.1 %shard_map.137 = (bf16[384,512]{1,0:T(8,128)(2,1)S(1)}, bf16[384,256]{1,0:T(8,128)(2,1)}) custom-call(s32[24]{0:T(128)S(1)} %concatenate.12.info, bf16[48,4096]{1,0:T(8,128)(2,1)S(1)} %collective-permute-done.3.refs_0_, bf16[48,4096]{1,0:T(8,128)(2,1)S(1)} %collective-permute-done.4.refs_1_, bf16[96,4096]{1,0:T(8,128)(2,1)S(1)} %collective-permute-done.5.refs_2_, ...), custom_call_target="tpu_custom_call" | custom-call | flops 3623878656 | bytes 12582912 | tf_op jit(solution)/shard_map/pallas_call | solution.py:106
  84.4 34.1 %all-gather.7.cloned.1.call-done = bf16[6144,256]{1,0:T(8,128)(2,1)} async-done(((bf16[384,256]{1,0:T(8,128)(2,1)}), bf16[6144,256]{1,0:T(8,128)(2,1)}) %all-gather.7.cloned.1.call-update) | async-done | bytes 3145744 | tf_op jit(solution)/shard_map/all_gather | solution.py:379
  118.5 1.9 copy-done
  120.4 17.0 %shard_map.140.mixed = bf16[384,512]{1,0:T(8,128)(2,1)S(1)} custom-call(s32[24]{0:T(128)S(1)} %concatenate.12.info, bf16[384,512]{1,0:T(8,128)(2,1)S(1)} %copy-done.13, bf16[384,512]{1,0:T(8,128)(2,1)S(1)} %get-tuple-element.18.q2, bf16[4,2,2,4,96,256]{5,4,3,2,1,0:T(8,128)(2,1)S(1)} %bitcast.18, bf16[4,2,2,4,96,256]{5,4,3,2,1,0:T(8,128)(2,1)} %bitcast.20), custom_call_target="tpu_custom_call" | custom-call | flops 9663676416 | bytes 8388608 | tf_op jit(solution)/shard_map/pallas_call | solution.py:232
  137.4 8.4 %shard_map.141 = (bf16[96,4096]{1,0:T(8,128)(2,1)S(1)}, bf16[96,4096]{1,0:T(8,128)(2,1)S(1)}, bf16[96,4096]{1,0:T(8,128)(2,1)S(1)}, bf16[96,4096]{1,0:T(8,128)(2,1)S(1)}) custom-call(s32[24]{0:T(128)S(1)} %concatenate.12.info, bf16[384,512]{1,0:T(8,128)(2,1)S(1)} %shard_map.140.mixed, bf16[512,4096]{1,0:T(8,128)(2,1)} %weight.3, ...), custom_call_target="tpu_custom_call" | custom-call | flops 2415919104 | bytes 8388608 | tf_op jit(solution)/shard_map/pallas_call | solution.py:283
  145.8 9.2 %collective-permute-start.8 = (bf16[96,4096]{1,0:T(8,128)(2,1)S(1)}, bf16[96,4096]{1,0:T(8,128)(2,1)S(1)}, u32[]{:S(2)}, u32[]{:S(2)}) collective-permute-start(bf16[96,4096]{1,0:T(8,128)(2,1)S(1)} %get-tuple-element.24), channel_id=1, source_target_pairs={{0,20},{1,21},{2,22},{3,23},{4,16},{5,17},{6,18},{7,19},{8,28},{9,... | collective-permute-start | bytes 2359304 | tf_op jit(solution)/shard_map/ppermute | solution.py:316
  155.0 24.1 %shard_map.138.mixed = bf16[384,512]{1,0:T(8,128)(2,1)S(1)} custom-call(s32[24]{0:T(128)S(1)} %concatenate.12.info, bf16[384,512]{1,0:T(8,128)(2,1)S(1)} %copy-done.13, bf16[384,512]{1,0:T(8,128)(2,1)S(1)} %get-tuple-element.18.q2, bf16[4,2,2,4,96,256]{5,4,3,2,1,0:T(8,128)(2,1)S(1)} %bitcast.19, bf16[4,2,2,4,96,256]{5,4,3,2,1,0:T(8,128)(2,1)} %bitcast.21), custom_call_target="tpu_custom_call" | custom-call | flops 9663676416 | bytes 8388608 | tf_op jit(solution)/shard_map/pallas_call | solution.py:232
  179.1 8.1 %shard_map.139 = (bf16[96,4096]{1,0:T(8,128)(2,1)S(1)}, bf16[96,4096]{1,0:T(8,128)(2,1)S(1)}, bf16[96,4096]{1,0:T(8,128)(2,1)S(1)}, bf16[96,4096]{1,0:T(8,128)(2,1)S(1)}) custom-call(s32[24]{0:T(128)S(1)} %concatenate.12.info, bf16[384,512]{1,0:T(8,128)(2,1)S(1)} %shard_map.138.mixed, bf16[512,4096]{1,0:T(8,128)(2,1)} %weight.3, ...), custom_call_target="tpu_custom_call" | custom-call | flops 2415919104 | bytes 8388608 | tf_op jit(solution)/shard_map/pallas_call | solution.py:283
  191.1 3.0 %collective-permute-start.11 = (bf16[48,4096]{1,0:T(8,128)(2,1)S(1)}, bf16[48,4096]{1,0:T(8,128)(2,1)S(1)}, u32[]{:S(2)}, u32[]{:S(2)}) collective-permute-start(bf16[48,4096]{1,0:T(8,128)(2,1)S(1)} %get-tuple-element.30), channel_id=1, source_target_pairs={{0,3},{1,0},{2,1},{3,2},{4,7},{5,4},{6,5},{7,6},{8,11},{9,8},{10,9... | collective-permute-start | bytes 1179656 | tf_op jit(solution)/shard_map/ppermute | solution.py:309
  194.1 9.8 %collective-permute-done.13 = bf16[96,4096]{1,0:T(8,128)(2,1)S(1)} collective-permute-done((bf16[96,4096]{1,0:T(8,128)(2,1)S(1)}, bf16[96,4096]{1,0:T(8,128)(2,1)S(1)}, u32[]{:S(2)}, u32[]{:S(2)}) %collective-permute-start.13) | collective-permute-done | bytes 786464 | tf_op jit(solution)/shard_map/ppermute | solution.py:309
  203.9 4.4 %collective-permute-done.14 = bf16[96,4096]{1,0:T(8,128)(2,1)S(1)} collective-permute-done((bf16[96,4096]{1,0:T(8,128)(2,1)S(1)}, bf16[96,4096]{1,0:T(8,128)(2,1)S(1)}, u32[]{:S(2)}, u32[]{:S(2)}) %collective-permute-start.14) | collective-permute-done | bytes 786464 | tf_op jit(solution)/shard_map/ppermute | solution.py:309
  208.7 4.7 %collective-permute-done.11 = bf16[48,4096]{1,0:T(8,128)(2,1)S(1)} collective-permute-done((bf16[48,4096]{1,0:T(8,128)(2,1)S(1)}, bf16[48,4096]{1,0:T(8,128)(2,1)S(1)}, u32[]{:S(2)}, u32[]{:S(2)}) %collective-permute-start.11) | collective-permute-done | bytes 393248 | tf_op jit(solution)/shard_map/ppermute | solution.py:309
  213.5 3.1 %collective-permute-start.12 = (bf16[96,4096]{1,0:T(8,128)(2,1)S(1)}, bf16[96,4096]{1,0:T(8,128)(2,1)S(1)}, u32[]{:S(2)}, u32[]{:S(2)}) collective-permute-start(bf16[96,4096]{1,0:T(8,128)(2,1)S(1)} %pad_maximum_fusion.2), channel_id=1, source_target_pairs={{0,3},{1,0},{2,1},{3,2},{4,7},{5,4},{6,5},{7,6},{8,11},{9,8},{10,9... | collective-permute-start | bytes 2359304 | tf_op jit(solution)/shard_map/ppermute | solution.py:309
  216.9 3.8 %collective-permute-done.15 = bf16[96,4096]{1,0:T(8,128)(2,1)S(1)} collective-permute-done((bf16[96,4096]{1,0:T(8,128)(2,1)S(1)}, bf16[96,4096]{1,0:T(8,128)(2,1)S(1)}, u32[]{:S(2)}, u32[]{:S(2)}) %collective-permute-start.15) | collective-permute-done | bytes 786464 | tf_op jit(solution)/shard_map/ppermute | solution.py:316
  220.6 5.5 %collective-permute-done.12 = bf16[96,4096]{1,0:T(8,128)(2,1)S(1)} collective-permute-done((bf16[96,4096]{1,0:T(8,128)(2,1)S(1)}, bf16[96,4096]{1,0:T(8,128)(2,1)S(1)}, u32[]{:S(2)}, u32[]{:S(2)}) %collective-permute-start.12) | collective-permute-done | bytes 786464 | tf_op jit(solution)/shard_map/ppermute | solution.py:309
  226.1 3.9 %collective-permute-done.10 = bf16[96,4096]{1,0:T(8,128)(2,1)S(1)} collective-permute-done((bf16[96,4096]{1,0:T(8,128)(2,1)S(1)}, bf16[96,4096]{1,0:T(8,128)(2,1)S(1)}, u32[]{:S(2)}, u32[]{:S(2)}) %collective-permute-start.10) | collective-permute-done | bytes 786464 | tf_op jit(solution)/shard_map/ppermute | solution.py:309
  (69 shorter events, 21.8 us)
Async XLA Ops:
  6.5 27.9 %copy-start.6 = (bf16[128,512]{1,0:T(8,128)(2,1)S(1)}, bf16[128,512]{1,0:T(8,128)(2,1)}, u32[]{:S(2)}) copy-start(bf16[128,512]{1,0:T(8,128)(2,1)} %refs_9_.3) | copy-start | bytes 393220
  6.5 27.9 %copy-start.2 = (bf16[4096,128]{1,0:T(8,128)(2,1)S(1)}, bf16[4096,128]{1,0:T(8,128)(2,1)}, u32[]{:S(2)}) copy-start(bf16[4096,128]{1,0:T(8,128)(2,1)} %refs_6_.3) | copy-start | bytes 3145732
  6.5 77.9 %all-gather.5.cloned.1.call-start = ((), (), s32[]{:S(2)}) async-start(), calls=%async_computation | async-start | bytes 3342336 | tf_op jit(solution)/shard_map/all_gather | solution.py:379
  9.5 19.6 %collective-permute-start.2 = (bf16[96,4096]{1,0:T(8,128)(2,1)S(1)}, bf16[96,4096]{1,0:T(8,128)(2,1)}, u32[]{:S(2)}, u32[]{:S(2)}) collective-permute-start(bf16[96,4096]{1,0:T(8,128)(2,1)S(1)} %fusion.2.refs_0_), channel_id=1, source_target_pairs={{0,20},{1,21},{2,22},{3,23},{4,16},{5,17},{6,18},{7,19},{8,28},{9,... | collective-permute-start | bytes 2359304 | tf_op jit(solution)/shard_map/ppermute | solution.py:316
  11.4 19.5 %collective-permute-start.1 = (bf16[96,4096]{1,0:T(8,128)(2,1)S(1)}, bf16[96,4096]{1,0:T(8,128)(2,1)S(1)}, u32[]{:S(2)}, u32[]{:S(2)}) collective-permute-start(bf16[96,4096]{1,0:T(8,128)(2,1)S(1)} %fusion.2.refs_0_), channel_id=1, source_target_pairs={{0,3},{1,0},{2,1},{3,2},{4,7},{5,4},{6,5},{7,6},{8,11},{9,8},{10,9... | collective-permute-start | bytes 2359304 | tf_op jit(solution)/shard_map/ppermute | solution.py:309
  14.5 19.9 %collective-permute-start = (bf16[96,4096]{1,0:T(8,128)(2,1)S(1)}, bf16[96,4096]{1,0:T(8,128)(2,1)S(1)}, u32[]{:S(2)}, u32[]{:S(2)}) collective-permute-start(bf16[96,4096]{1,0:T(8,128)(2,1)S(1)} %fusion.2.refs_0_), channel_id=1, source_target_pairs={{0,1},{1,2},{2,3},{3,0},{4,5},{5,6},{6,7},{7,4},{8,9},{9,10},{10,1... | collective-permute-start | bytes 2359304 | tf_op jit(solution)/shard_map/ppermute | solution.py:309
  47.0 28.2 %copy-start.9 = (bf16[128,128]{1,0:T(8,128)(2,1)S(1)}, bf16[128,128]{1,0:T(8,128)(2,1)}, u32[]{:S(2)}) copy-start(bf16[128,128]{1,0:T(8,128)(2,1)} %refs_10_.3) | copy-start | bytes 98308
  47.1 28.2 %copy-start.11 = (bf16[128,128]{1,0:T(8,128)(2,1)S(1)}, bf16[128,128]{1,0:T(8,128)(2,1)}, u32[]{:S(2)}) copy-start(bf16[128,128]{1,0:T(8,128)(2,1)} %refs_11_.1) | copy-start | bytes 98308
  47.1 71.4 %all-gather.7.cloned.1.call-start = ((), (), s32[]{:S(2)}) async-start(), calls=%async_computation.1 | async-start | bytes 3342336 | tf_op jit(solution)/shard_map/all_gather | solution.py:379
  47.1 28.1 %copy-start.4 = (bf16[4096,128]{1,0:T(8,128)(2,1)S(1)}, bf16[4096,128]{1,0:T(8,128)(2,1)}, u32[]{:S(2)}) copy-start(bf16[4096,128]{1,0:T(8,128)(2,1)} %refs_7_.3) | copy-start | bytes 3145732
  47.2 12.1 %collective-permute-start.4 = (bf16[48,4096]{1,0:T(8,128)(2,1)S(1)}, bf16[48,4096]{1,0:T(8,128)(2,1)S(1)}, u32[]{:S(2)}, u32[]{:S(2)}) collective-permute-start(bf16[48,4096]{1,0:T(8,128)(2,1)S(1)} %slice.33), channel_id=1, source_target_pairs={{0,3},{1,0},{2,1},{3,2},{4,7},{5,4},{6,5},{7,6},{8,11},{9,8},{10,9... | collective-permute-start | bytes 1179656 | tf_op jit(solution)/shard_map/ppermute | solution.py:309
  47.5 13.3 %collective-permute-start.3 = (bf16[48,4096]{1,0:T(8,128)(2,1)S(1)}, bf16[48,4096]{1,0:T(8,128)(2,1)S(1)}, u32[]{:S(2)}, u32[]{:S(2)}) collective-permute-start(bf16[48,4096]{1,0:T(8,128)(2,1)S(1)} %slice.32), channel_id=1, source_target_pairs={{0,1},{1,2},{2,3},{3,0},{4,5},{5,6},{6,7},{7,4},{8,9},{9,10},{10,1... | collective-permute-start | bytes 1179656 | tf_op jit(solution)/shard_map/ppermute | solution.py:309
  49.4 24.1 %collective-permute-start.6 = (bf16[96,4096]{1,0:T(8,128)(2,1)}, bf16[96,4096]{1,0:T(8,128)(2,1)S(1)}, u32[]{:S(2)}, u32[]{:S(2)}) collective-permute-start(bf16[96,4096]{1,0:T(8,128)(2,1)} %collective-permute-done.2.refs_3_), channel_id=1, source_target_pairs={{0,3},{1,0},{2,1},{3,2},{4,7},{5,4},{6,5},{7,6},{8,11},{9,8},{10,9... | collective-permute-start | bytes 2359304 | tf_op jit(solution)/shard_map/ppermute | solution.py:309
  50.9 24.2 %collective-permute-start.5 = (bf16[96,4096]{1,0:T(8,128)(2,1)}, bf16[96,4096]{1,0:T(8,128)(2,1)S(1)}, u32[]{:S(2)}, u32[]{:S(2)}) collective-permute-start(bf16[96,4096]{1,0:T(8,128)(2,1)} %collective-permute-done.2.refs_3_), channel_id=1, source_target_pairs={{0,1},{1,2},{2,3},{3,0},{4,5},{5,6},{6,7},{7,4},{8,9},{9,10},{10,1... | collective-permute-start | bytes 2359304 | tf_op jit(solution)/shard_map/ppermute | solution.py:309
  60.9 57.5 %copy-start.13 = (bf16[384,512]{1,0:T(8,128)(2,1)S(1)}, bf16[384,512]{1,0:T(8,128)(2,1)}, u32[]{:S(2)}) copy-start(bf16[384,512]{1,0:T(8,128)(2,1)} %copy-done.12) | copy-start | bytes 1179652
  61.0 14.3 %collective-permute-start.7 = (bf16[96,4096]{1,0:T(8,128)(2,1)S(1)}, bf16[96,4096]{1,0:T(8,128)(2,1)S(1)}, u32[]{:S(2)}, u32[]{:S(2)}) collective-permute-start(bf16[96,4096]{1,0:T(8,128)(2,1)S(1)} %pad_maximum_fusion), channel_id=1, source_target_pairs={{0,20},{1,21},{2,22},{3,23},{4,16},{5,17},{6,18},{7,19},{8,28},{9,... | collective-permute-start | bytes 2359304 | tf_op jit(solution)/shard_map/ppermute | solution.py:316
  145.8 44.8 %collective-permute-start.8 = (bf16[96,4096]{1,0:T(8,128)(2,1)S(1)}, bf16[96,4096]{1,0:T(8,128)(2,1)S(1)}, u32[]{:S(2)}, u32[]{:S(2)}) collective-permute-start(bf16[96,4096]{1,0:T(8,128)(2,1)S(1)} %get-tuple-element.24), channel_id=1, source_target_pairs={{0,20},{1,21},{2,22},{3,23},{4,16},{5,17},{6,18},{7,19},{8,28},{9,... | collective-permute-start | bytes 2359304 | tf_op jit(solution)/shard_map/ppermute | solution.py:316
  187.3 16.7 %collective-permute-start.13 = (bf16[96,4096]{1,0:T(8,128)(2,1)S(1)}, bf16[96,4096]{1,0:T(8,128)(2,1)S(1)}, u32[]{:S(2)}, u32[]{:S(2)}) collective-permute-start(bf16[96,4096]{1,0:T(8,128)(2,1)S(1)} %get-tuple-element.27), channel_id=1, source_target_pairs={{0,1},{1,2},{2,3},{3,0},{4,5},{5,6},{6,7},{7,4},{8,9},{9,10},{10,1... | collective-permute-start | bytes 2359304 | tf_op jit(solution)/shard_map/ppermute | solution.py:309
  188.7 19.5 %collective-permute-start.14 = (bf16[96,4096]{1,0:T(8,128)(2,1)S(1)}, bf16[96,4096]{1,0:T(8,128)(2,1)S(1)}, u32[]{:S(2)}, u32[]{:S(2)}) collective-permute-start(bf16[96,4096]{1,0:T(8,128)(2,1)S(1)} %get-tuple-element.28), channel_id=1, source_target_pairs={{0,3},{1,0},{2,1},{3,2},{4,7},{5,4},{6,5},{7,6},{8,11},{9,8},{10,9... | collective-permute-start | bytes 2359304 | tf_op jit(solution)/shard_map/ppermute | solution.py:309
  190.8 25.8 %collective-permute-start.9 = (bf16[48,4096]{1,0:T(8,128)(2,1)S(1)}, bf16[48,4096]{1,0:T(8,128)(2,1)S(1)}, u32[]{:S(2)}, u32[]{:S(2)}) collective-permute-start(bf16[48,4096]{1,0:T(8,128)(2,1)S(1)} %get-tuple-element.29), channel_id=1, source_target_pairs={{0,1},{1,2},{2,3},{3,0},{4,5},{5,6},{6,7},{7,4},{8,9},{9,10},{10,1... | collective-permute-start | bytes 1179656 | tf_op jit(solution)/shard_map/ppermute | solution.py:309
  191.1 22.3 %collective-permute-start.11 = (bf16[48,4096]{1,0:T(8,128)(2,1)S(1)}, bf16[48,4096]{1,0:T(8,128)(2,1)S(1)}, u32[]{:S(2)}, u32[]{:S(2)}) collective-permute-start(bf16[48,4096]{1,0:T(8,128)(2,1)S(1)} %get-tuple-element.30), channel_id=1, source_target_pairs={{0,3},{1,0},{2,1},{3,2},{4,7},{5,4},{6,5},{7,6},{8,11},{9,8},{10,9... | collective-permute-start | bytes 1179656 | tf_op jit(solution)/shard_map/ppermute | solution.py:309
  208.6 12.1 %collective-permute-start.15 = (bf16[96,4096]{1,0:T(8,128)(2,1)S(1)}, bf16[96,4096]{1,0:T(8,128)(2,1)S(1)}, u32[]{:S(2)}, u32[]{:S(2)}) collective-permute-start(bf16[96,4096]{1,0:T(8,128)(2,1)S(1)} %add_convert_fusion.1), channel_id=1, source_target_pairs={{0,20},{1,21},{2,22},{3,23},{4,16},{5,17},{6,18},{7,19},{8,28},{9,... | collective-permute-start | bytes 2359304 | tf_op jit(solution)/shard_map/ppermute | solution.py:316
  213.5 12.6 %collective-permute-start.12 = (bf16[96,4096]{1,0:T(8,128)(2,1)S(1)}, bf16[96,4096]{1,0:T(8,128)(2,1)S(1)}, u32[]{:S(2)}, u32[]{:S(2)}) collective-permute-start(bf16[96,4096]{1,0:T(8,128)(2,1)S(1)} %pad_maximum_fusion.2), channel_id=1, source_target_pairs={{0,3},{1,0},{2,1},{3,2},{4,7},{5,4},{6,5},{7,6},{8,11},{9,8},{10,9... | collective-permute-start | bytes 2359304 | tf_op jit(solution)/shard_map/ppermute | solution.py:309
  216.8 13.3 %collective-permute-start.10 = (bf16[96,4096]{1,0:T(8,128)(2,1)S(1)}, bf16[96,4096]{1,0:T(8,128)(2,1)S(1)}, u32[]{:S(2)}, u32[]{:S(2)}) collective-permute-start(bf16[96,4096]{1,0:T(8,128)(2,1)S(1)} %pad_maximum_fusion.1), channel_id=1, source_target_pairs={{0,1},{1,2},{2,3},{3,0},{4,5},{5,6},{6,7},{7,4},{8,9},{9,10},{10,1... | collective-permute-start | bytes 2359304 | tf_op jit(solution)/shard_map/ppermute | solution.py:309
  (9 other events, 66.1 us)
Sparse Core Ops, SparseCore 0:
  47.2 32.0 all-gather.4
  84.5 33.9 all-gather.6
